TPU v7x, 32 devices: a whole 2x2x4 slice. The times are simulated.
32 devices in a mesh: rep: 2 (over y), ep: 4 (over z), tp: 4 (over x, core).
Axes of the slice: x: 2, y: 2, z: 4, core: 2. Of those that a mesh axis runs over, the one named last changes fastest.
Arguments:
- hidden_in: bfloat16 [256, 4096], P(('rep', 'ep')), parts along dimension 0
- queries: bfloat16 [256, 32, 128], P(('rep', 'ep'), 'tp'), parts along dimension 0
- new_keys: bfloat16 [256, 8, 128], P(('rep', 'ep'), 'tp'), parts along dimension 0, may hold values from -6 to 6
- new_values: bfloat16 [256, 8, 128], P(('rep', 'ep'), 'tp'), parts along dimension 0, may hold values from -6 to 6
- key_cache: bfloat16 [256, 8, 256, 128], P(('rep', 'ep'), 'tp'), parts along dimension 0
- value_cache: bfloat16 [256, 8, 256, 128], P(('rep', 'ep'), 'tp'), parts along dimension 0, may hold values from -6 to 6
- lengths: int32 [256], P(('rep', 'ep')), parts along dimension 0, may hold values from 2 to 256
- out_weight: bfloat16 [4096, 4096], P('tp'), may hold values from -0.09375 to 0.09375
- norm_gain: bfloat16 [4096], replicated, may hold values from 0.099609375 to 1.8984375
- router_weight: bfloat16 [4096, 16], replicated, may hold values from -0.1875 to 0.1875
- latent_down: bfloat16 [4096, 1024], P(None, 'tp'), may hold values from -0.09375 to 0.09375
- latent_up: bfloat16 [1024, 4096], P('tp'), may hold values from -0.375 to 0.375
- gate_weight: bfloat16 [16, 1024, 1536], P('ep', None, 'tp'), may hold values from -0.1875 to 0.1875
- up_weight: bfloat16 [16, 1024, 1536], P('ep', None, 'tp'), may hold values from -0.1875 to 0.1875
- down_weight: bfloat16 [16, 1536, 1024], P('ep', 'tp'), may hold values from -0.625 to 0.625
- routes: int32 [256, 16], P('rep'), parts along dimension 0, may hold values from 0 to 15, as said below
- slot_index: int32 [256, 16], P('rep'), parts along dimension 0, may hold values from 0 to 127, as said below
Outputs:
- layer_out: bfloat16 [256, 4096], P(('rep', 'ep', 'tp')), parts along dimension 0
There are 2 independent parts, one for each index of `rep`. A program takes and returns all parts, laid end to end along the dimension named above; an argument that names none is the same for every part. Nothing has to cross between parts.
Inputs may be any that keep to these rules, and one draw needn't show every extreme that they name: `routes`: each row names 16 different experts; one expert, drawn from the seed, is named by every row. slot_index[s,k] counts the rows that name routes[s,k] and come before s in an order of the rows drawn from the seed, so the slots of one expert are distinct; a choice with a slot of 256 or more is dropped.
All inputs are finite; a program needn't handle non-finite values.
Results may differ from a plain program's by a relative error of at most 0.018.
Values may be sent and summed in bfloat16 or wider, within the bound.
A program may use at most 128 MiB of HBM per device.

v0:
```python
import math

import jax
import jax.numpy as jnp
from jax import lax
from jax.sharding import PartitionSpec as P


def attention(queries, new_keys, new_values, key_cache, value_cache, lengths):
    rows, heads, width = queries.shape
    kv_heads = new_keys.shape[1]
    grouped = queries.reshape(rows, kv_heads, heads // kv_heads, width)
    scale = 1.0 / math.sqrt(width)
    cached = (
        jnp.einsum("skgd,skpd->skgp", grouped, key_cache, preferred_element_type=jnp.float32)
        * scale
    )
    own = jnp.einsum("skgd,skd->skg", grouped, new_keys, preferred_element_type=jnp.float32) * scale
    valid = jnp.arange(key_cache.shape[2], dtype=jnp.int32)[None, :] < lengths[:, None]
    cached = jnp.where(valid[:, None, None, :], cached, -jnp.inf)
    top = jnp.maximum(jnp.max(cached, axis=-1), own)
    expos = jnp.exp(cached - top[..., None])
    own_expo = jnp.exp(own - top)
    total = jnp.sum(expos, axis=-1) + own_expo
    probs = (expos / total[..., None]).astype(jnp.bfloat16)
    own_probs = (own_expo / total).astype(jnp.bfloat16)
    mixed = jnp.einsum("skgp,skpd->skgd", probs, value_cache, preferred_element_type=jnp.float32)
    mixed = (
        mixed
        + own_probs.astype(jnp.float32)[..., None] * new_values.astype(jnp.float32)[:, :, None, :]
    )
    return mixed.reshape(rows, heads * width).astype(jnp.bfloat16)


def rms_norm(values, norm_gain):
    mean_sq = jnp.mean(values * values, axis=-1, keepdims=True)
    return (values * lax.rsqrt(mean_sq + 1e-05) * norm_gain.astype(jnp.float32)).astype(
        jnp.bfloat16
    )


def on_device(
    hidden_in,
    queries,
    new_keys,
    new_values,
    key_cache,
    value_cache,
    lengths,
    out_weight,
    norm_gain,
    router_weight,
    latent_down,
    latent_up,
    gate_weight,
    up_weight,
    down_weight,
    routes,
    slot_index,
):
    tok_block = queries.shape[0]
    tp_count = lax.axis_size("tp")
    ep_count = lax.axis_size("ep")
    tp_rank = lax.axis_index("tp")
    ep_rank = lax.axis_index("ep")
    tok_dev = tok_block // tp_count
    lat_local = latent_down.shape[1]
    exp_dev = gate_weight.shape[0]
    experts_all = router_weight.shape[1]
    tok_total = routes.shape[0]
    slots_all = 2 * tok_total * routes.shape[1] // experts_all
    attended = attention(queries, new_keys, new_values, key_cache, value_cache, lengths)
    summed = lax.psum_scatter(
        jnp.dot(attended, out_weight, preferred_element_type=jnp.float32),
        "tp",
        scatter_dimension=0,
        tiled=True,
    )
    own_rows = lax.dynamic_slice_in_dim(hidden_in, tp_rank * tok_dev, tok_dev, 0)
    residual = own_rows.astype(jnp.float32) + summed
    normed = rms_norm(residual, norm_gain)
    piece = lax.all_gather(normed, "tp", axis=0, tiled=True)
    joined = jnp.concatenate(
        [
            jnp.dot(piece, latent_down, preferred_element_type=jnp.float32),
            jnp.dot(piece, router_weight, preferred_element_type=jnp.float32),
        ],
        axis=1,
    )
    latent_part = joined[:, :lat_local]
    logits = joined[:, lat_local:]
    latent_cols = latent_part.astype(jnp.bfloat16)
    gates = jax.nn.sigmoid(logits)
    block_routes = lax.dynamic_slice_in_dim(routes, ep_rank * tok_block, tok_block, 0)
    block_slots = lax.dynamic_slice_in_dim(slot_index, ep_rank * tok_block, tok_block, 0)
    ident = jnp.arange(experts_all, dtype=jnp.int32)
    chosen = block_routes[:, :, None] == ident[None, None, :]
    picked = jnp.sum(chosen, axis=1).astype(jnp.float32)
    kept = jnp.sum(chosen & (block_slots[:, :, None] < slots_all), axis=1).astype(jnp.float32)
    weights = kept * gates / jnp.sum(picked * gates, axis=-1, keepdims=True)
    local_ids = ep_rank * exp_dev + jnp.arange(exp_dev, dtype=jnp.int32)
    matches = routes[:, :, None] == local_ids[None, None, :]
    slot_tok = jnp.sum(jnp.where(matches, slot_index[:, :, None], 0), axis=1)
    slot_tok = jnp.where(jnp.any(matches, axis=1), slot_tok, slots_all)
    placing = (
        slot_tok.T[:, None, :] == jnp.arange(slots_all, dtype=jnp.int32)[None, :, None]
    ).astype(jnp.bfloat16)
    latent_full = lax.all_gather(latent_cols, "tp", axis=1, tiled=True)
    filled = jnp.einsum(
        "jct,tl->jcl",
        placing,
        lax.all_gather(latent_full, "ep", axis=0, tiled=True),
        preferred_element_type=jnp.float32,
    ).astype(jnp.bfloat16)
    gate = jnp.einsum("jcl,jlf->jcf", filled, gate_weight, preferred_element_type=jnp.float32)
    upper = jnp.einsum("jcl,jlf->jcf", filled, up_weight, preferred_element_type=jnp.float32)
    active = (jax.nn.silu(gate) * upper).astype(jnp.bfloat16)
    outputs = lax.psum_scatter(
        jnp.einsum("jcf,jfl->ljc", active, down_weight, preferred_element_type=jnp.float32)
        .reshape(lat_local * lax.axis_size("tp"), exp_dev * slots_all)
        .astype(jnp.bfloat16),
        "tp",
        scatter_dimension=0,
        tiled=True,
    ).astype(jnp.float32)
    outputs = outputs.astype(jnp.bfloat16).reshape(lat_local, exp_dev, slots_all)
    returned = jnp.einsum(
        "jcg,ljc->jgl", placing, outputs, preferred_element_type=jnp.float32
    ).astype(jnp.bfloat16)
    returned = returned.reshape(exp_dev, ep_count, tok_block, lat_local)
    came_back = lax.all_to_all(returned, "ep", split_axis=1, concat_axis=1, tiled=True)
    combine_w = weights.reshape(tok_block, ep_count, exp_dev)
    combined = jnp.einsum("sej,jesl->sl", combine_w, came_back.astype(jnp.float32)).astype(
        jnp.bfloat16
    )
    lifted = lax.psum_scatter(
        jnp.dot(combined, latent_up, preferred_element_type=jnp.float32).astype(jnp.bfloat16),
        "tp",
        scatter_dimension=0,
        tiled=True,
    ).astype(jnp.float32)
    return (residual + lifted).astype(jnp.bfloat16)


def solution(mesh):
    return jax.shard_map(
        on_device,
        mesh=mesh,
        in_specs=(
            P(("rep", "ep"), None),
            P(("rep", "ep"), "tp", None),
            P(("rep", "ep"), "tp", None),
            P(("rep", "ep"), "tp", None),
            P(("rep", "ep"), "tp", None, None),
            P(("rep", "ep"), "tp", None, None),
            P(("rep", "ep")),
            P("tp", None),
            P(),
            P(),
            P(None, "tp"),
            P("tp", None),
            P("ep", None, "tp"),
            P("ep", None, "tp"),
            P("ep", "tp", None),
            P("rep", None),
            P("rep", None),
        ),
        out_specs=P(("rep", "ep", "tp"), None),
        check_vma=False,
    )
```

profile of v0, /device:TPU:0, one launch (start us, length us, event | category | flops | bytes accessed | tf_op | source)
XLA Modules:
  0.0 167.2 jit_solution(17693762096494919266)
XLA Ops:
  6.5 0.9 iota_compare_fusion.4
  7.4 1.1 fusion.16
  8.6 0.7 convert_element_type.80
  9.4 3.5 %fusion.22 = (f32[32,2,4]{2,1,0:T(2,128)S(1)}, f32[32,2,4,256]{3,2,1,0:T(4,128)S(1)}) fusion(bf16[32,2,4,128]{3,2,1,0:T(4,128)(2,1)} %bitcast.56, bf16[32,2,256,128]{3,2,1,0:T(8,128)(2,1)} %param.21, pred[32,256]{1,0:T(8,128)(4,1)S(1)} %iota_compare_fusion.4), kind=kOutput, calls=%fused_computation.55 | convolution fusion | flops 16973568 | bytes 4531200 | tf_op jit(solution)/shard_map/skgd,skpd->skgp/dot_general | solution.py:15
  13.0 0.1 copy.46
  13.1 0.3 fusion.11
  13.5 0.7 copy.49
  14.2 0.7 copy.48
  14.9 2.9 %fusion.1 = bf16[32,2,4,128]{3,2,1,0:T(4,128)(2,1)S(1)} fusion(bf16[32,2,256,128]{3,2,1,0:T(8,128)(2,1)} %param.22, f32[32,2,4,256]{3,2,1,0:T(4,128)S(1)} %get-tuple-element.10, f32[32,2,4]{2,1,0:T(2,128)} %copy.48, f32[32,2,4]{2,1,0:T(2,128)S(1)} %copy.46, f32[32,2,128]{2,1,0:T(2,128)S(1)} %convert_element_type.80, f32[32,2,4]{2,1,0:T(2,128)} %copy.49), kind=kOutput, calls=%fused_computation.8 | convolution fusion | flops 17072128 | bytes 4557824 | tf_op jit(solution)/shard_map/skgp,skpd->skgd/dot_general | solution.py:27
  17.9 5.8 %fusion.23 = f32[32,4096]{1,0:T(8,128)} fusion(bf16[32,1024]{1,0:T(8,128)(2,1)S(1)} %convert_element_type.82, bf16[1024,4096]{1,0:T(8,128)(2,1)} %param.24), kind=kOutput, calls=%fused_computation.56 | convolution fusion | flops 268435456 | bytes 8978432 | tf_op jit(solution)/shard_map/dot_general | solution.py:74
  24.0 24.2 %reduce-scatter.4.cloned.1.call-done = f32[8,4096]{1,0:T(8,128)} async-done(((f32[32,4096]{1,0:T(8,128)}), f32[8,4096]{1,0:T(8,128)}) %reduce-scatter.4.cloned.1.call-update) | async-done | bytes 131088 | tf_op jit(solution)/shard_map/reduce_scatter | solution.py:73
  48.2 1.1 multiply_reduce_fusion
  49.3 1.0 multiply_convert_fusion.1
  50.3 5.8 %all_gather.9 = bf16[32,4096]{1,0:T(8,128)(2,1)S(1)} all-gather(bf16[8,4096]{1,0:T(8,128)(2,1)S(1)} %multiply_convert_fusion.1), channel_id=1, replica_groups=mesh['rep'=2,'ep'=4,'tp'=4] {'tp'}, dimensions={0}, use_global_device_ids=true | all-gather | bytes 327680 | tf_op jit(solution)/shard_map/all_gather | solution.py:82
  56.0 2.2 %convolution_convert_fusion.4 = bf16[32,256]{1,0:T(8,128)(2,1)S(1)} fusion(bf16[32,4096]{1,0:T(8,128)(2,1)S(1)} %all_gather.9, bf16[4096,256]{1,0:T(8,128)(2,1)} %param.27), kind=kOutput, calls=%fused_computation.9 | convolution fusion | flops 67117056 | bytes 2375680 | tf_op jit(solution)/shard_map/dot_general | solution.py:85
  58.2 5.2 %all_gather.10 = bf16[32,1024]{1,0:T(8,128)(2,1)S(1)} all-gather(bf16[32,256]{1,0:T(8,128)(2,1)S(1)} %convolution_convert_fusion.4), channel_id=1, replica_groups=mesh['rep'=2,'ep'=4,'tp'=4] {'tp'}, dimensions={1}, use_global_device_ids=true | all-gather | bytes 81920 | tf_op jit(solution)/shard_map/all_gather | solution.py:108
  63.5 14.0 %all_gather.11 = bf16[128,1024]{1,0:T(8,128)(2,1)S(1)} all-gather(bf16[32,1024]{1,0:T(8,128)(2,1)S(1)} %all_gather.10), channel_id=1, replica_groups=mesh['rep'=2,'ep'=4,'tp'=4] {'ep'}, dimensions={0}, use_global_device_ids=true | all-gather | bytes 327680 | tf_op jit(solution)/shard_map/all_gather | solution.py:112
  77.5 0.9 convolution_convert_fusion.2
  78.4 1.3 copy-done.1
  79.6 2.4 %fusion.24 = f32[4,256,384]{2,1,0:T(8,128)} fusion(bf16[4,256,1024]{2,1,0:T(8,128)(2,1)S(1)} %convolution_convert_fusion.2, bf16[4,1024,384]{2,1,0:T(8,128)(2,1)S(1)} %copy-done.2), kind=kOutput, calls=%fused_computation.57 | convolution fusion | flops 805306368 | bytes 6815744 | tf_op jit(solution)/shard_map/jcl,jlf->jcf/dot_general | solution.py:115
  82.1 6.7 %convolution_convert_fusion.1 = bf16[4,256,1024]{2,1,0:T(8,128)(2,1)} fusion(bf16[4,384,1024]{2,1,0:T(8,128)(2,1)S(1)} %copy-done, f32[4,256,384]{2,1,0:T(8,128)} %fusion.24, bf16[4,256,1024]{2,1,0:T(8,128)(2,1)} %copy-done.1, bf16[4,1024,384]{2,1,0:T(8,128)(2,1)} %param.30), kind=kOutput, calls=%fused_computation.1 | convolution fusion | flops 1614020608 | bytes 12058624 | tf_op jit(solution)/shard_map/jcf,jfl->ljc/dot_general | solution.py:119
  89.0 31.9 %reduce-scatter.6.cloned.1.call-done = bf16[256,1024]{0,1:T(8,128)(2,1)} async-done(((bf16[1024,1024]{0,1:T(8,128)(2,1)}), bf16[256,1024]{0,1:T(8,128)(2,1)}) %reduce-scatter.6.cloned.1.call-update) | async-done | bytes 524304 | tf_op jit(solution)/shard_map/reduce_scatter | solution.py:118
  121.0 1.3 convolution_convert_fusion.3
  122.3 0.7 copy.52
  123.0 4.6 %all-to-all-start = ((bf16[4,4,32,256]{3,2,0,1:T(8,128)(2,1)}), bf16[4,4,32,256]{3,2,0,1:T(8,128)(2,1)}, u32[]{:S(2)}, u32[]{:S(2)}) async-start(bf16[4,4,32,256]{3,2,0,1:T(8,128)(2,1)} %copy.52), calls=%async_computation.2 | async-start | bytes 524288 | tf_op jit(solution)/shard_map/all_to_all | solution.py:131
  127.6 1.1 multiply_reduce_fusion.1
  128.8 0.1 copy.57
  128.9 7.7 %all-to-all-done = bf16[4,4,32,256]{3,2,0,1:T(8,128)(2,1)} async-done(((bf16[4,4,32,256]{3,2,0,1:T(8,128)(2,1)}), bf16[4,4,32,256]{3,2,0,1:T(8,128)(2,1)}, u32[]{:S(2)}, u32[]{:S(2)}) %all-to-all-start) | async-done | bytes 262176 | tf_op jit(solution)/shard_map/all_to_all | solution.py:131
  136.6 1.4 fusion.9
  138.1 2.8 %convolution_convert_fusion = bf16[32,4096]{1,0:T(8,128)(2,1)} fusion(bf16[256,4096]{1,0:T(8,128)(2,1)} %param.28, bf16[32,1,256,1]{2,1,3,0:T(2,128)(2,1)S(1)} %fusion.9), kind=kOutput, calls=%fused_computation | convolution fusion | flops 67239936 | bytes 2375680 | tf_op jit(solution)/shard_map/dot_general | solution.py:137
  140.8 18.3 %reduce-scatter.8.cloned.1.call-done = bf16[8,4096]{1,0:T(8,128)(2,1)} async-done(((bf16[32,4096]{1,0:T(8,128)(2,1)}), bf16[8,4096]{1,0:T(8,128)(2,1)}) %reduce-scatter.8.cloned.1.call-update) | async-done | bytes 65552 | tf_op jit(solution)/shard_map/reduce_scatter | solution.py:136
  159.1 1.5 add_convert_fusion
  (37 shorter events, 0.9 us)
Async XLA Ops:
  6.5 75.5 %copy-start = (bf16[4,384,1024]{2,1,0:T(8,128)(2,1)S(1)}, bf16[4,384,1024]{2,1,0:T(8,128)(2,1)}, u32[]{:S(2)}) copy-start(bf16[4,384,1024]{2,1,0:T(8,128)(2,1)} %param.31) | copy-start | bytes 9437188
  6.5 41.7 %reduce-scatter.4.cloned.1.call-start = ((), (), s32[]{:S(2)}) async-start(), calls=%async_computation.4 | async-start | bytes 655360 | tf_op jit(solution)/shard_map/reduce_scatter | solution.py:73
  17.9 5.9 %copy-start.7 = (bf16[4096]{0:T(1024)(128)(2,1)S(1)}, bf16[4096]{0:T(1024)(128)(2,1)}, u32[]{:S(2)}) copy-start(bf16[4096]{0:T(1024)(128)(2,1)} %param.25) | copy-start | bytes 24580
  17.9 5.9 %copy-start.5 = (s32[128,16]{0,1:T(8,128)S(1)}, s32[128,16]{0,1:T(8,128)}, u32[]{:S(2)}) copy-start(s32[128,16]{0,1:T(8,128)} %param.32) | copy-start | bytes 24580
  17.9 6.0 %copy-start.6 = (s32[128,16]{0,1:T(8,128)S(1)}, s32[128,16]{0,1:T(8,128)}, u32[]{:S(2)}) copy-start(s32[128,16]{0,1:T(8,128)} %param.33) | copy-start | bytes 24580
  17.9 30.3 %copy-start.4 = (bf16[32,4096]{1,0:T(8,128)(2,1)S(1)}, bf16[32,4096]{1,0:T(8,128)(2,1)}, u32[]{:S(2)}) copy-start(bf16[32,4096]{1,0:T(8,128)(2,1)} %param.17) | copy-start | bytes 786436
  23.7 97.3 %reduce-scatter.6.cloned.1.call-start = ((), (), s32[]{:S(2)}) async-start(), calls=%async_computation.5 | async-start | bytes 2621440 | tf_op jit(solution)/shard_map/reduce_scatter | solution.py:118
  56.0 23.6 %copy-start.2 = (bf16[4,1024,384]{2,1,0:T(8,128)(2,1)S(1)}, bf16[4,1024,384]{2,1,0:T(8,128)(2,1)}, u32[]{:S(2)}) copy-start(bf16[4,1024,384]{2,1,0:T(8,128)(2,1)} %param.29) | copy-start | bytes 9437188
  78.3 1.3 copy-start.1
  123.0 13.6 %all-to-all-start = ((bf16[4,4,32,256]{3,2,0,1:T(8,128)(2,1)}), bf16[4,4,32,256]{3,2,0,1:T(8,128)(2,1)}, u32[]{:S(2)}, u32[]{:S(2)}) async-start(bf16[4,4,32,256]{3,2,0,1:T(8,128)(2,1)} %copy.52), calls=%async_computation.2 | async-start | bytes 524288 | tf_op jit(solution)/shard_map/all_to_all | solution.py:131
  127.6 31.5 %copy-start.3 = (f32[8,4096]{1,0:T(8,128)S(1)}, f32[8,4096]{1,0:T(8,128)}, u32[]{:S(2)}) copy-start(f32[8,4096]{1,0:T(8,128)} %reduce-scatter.4.cloned.1.call-done) | copy-start | bytes 393220
  127.6 31.5 %reduce-scatter.8.cloned.1.call-start = ((), (), s32[]{:S(2)}) async-start(), calls=%async_computation.6 | async-start | bytes 327680 | tf_op jit(solution)/shard_map/reduce_scatter | solution.py:136
Sparse Core Ops, SparseCore 0:
  23.8 24.3 reduce-scatter.3
  88.9 31.9 reduce-scatter.5
  141.0 18.1 reduce-scatter.7
where the time goes:
time: 168 us; the launch traced here: 167 us
  waiting for transfers between devices  82.2 us (49%)
  matrix products  32.2 us (19%)
  blocking collectives  25 us (15%)
  between operations  13.3 us (8%)
  other arithmetic  5.82 us (3%)
  starting transfers between devices  4.67 us (3%)
  local copies, waits for them, and re-layouts  4.08 us (2%)
    reduce_scatter x1, waiting for transfers between devices, on_device(): lax.psum_scatter(jnp.einsum('jcf,jfl->ljc', active, down_weight, preferre...  31.9 us
    reduce_scatter x1, waiting for transfers between devices, on_device(): lax.psum_scatter(jnp.dot(attended, out_weight, preferred_element_type=jnp...  24.2 us
    reduce_scatter x1, waiting for transfers between devices, on_device(): lax.psum_scatter(jnp.dot(combined, latent_up, preferred_element_type=jnp....  18.3 us
    all_gather x1, blocking collectives, on_device(): lax.all_gather(latent_full, 'ep', axis=0, tiled=True)  14 us
    all_to_all x1, waiting for transfers between devices, on_device(): lax.all_to_all(returned, 'ep', split_axis=1, concat_axis=1, tiled=True)  7.7 us
    dot_general x1, matrix products, on_device(): jnp.einsum('jcf,jfl->ljc', active, down_weight, preferred_element_type=jn...  6.71 us
    all_gather x1, blocking collectives, on_device(): piece = lax.all_gather(normed, 'tp', axis=0, tiled=True)  5.79 us
    dot_general x1, matrix products, on_device(): jnp.dot(attended, out_weight, preferred_element_type=jnp.float32)  5.77 us
  transfers between devices with their start and end apart: 4, of which 4 were waited for; matrix products, arithmetic and copies ran while one was open for 1% of the time, Pallas kernels for 0%

commit v1 on v0

v1 whole, which is shorter than its diff:
```python
import functools
import math

import jax
import jax.numpy as jnp
from jax import lax
from jax.experimental import pallas as pl
from jax.experimental.pallas import tpu as pltpu
from jax.sharding import PartitionSpec as P

MESH = pl.DeviceIdType.MESH
F32 = jnp.float32
BF16 = jnp.bfloat16


def dot(a, b):
    return jnp.dot(a, b, preferred_element_type=F32)


def dot_nt(a, b):
    return lax.dot_general(a, b, (((1,), (1,)), ((), ())), preferred_element_type=F32)


def layer_kernel(
    dims,
    hidden_ref,
    q_ref,
    nk_ref,
    nv_ref,
    k_hbm,
    v_hbm,
    len_ref,
    wo_hbm,
    gain_ref,
    router_hbm,
    wd_hbm,
    wu_hbm,
    wg_hbm,
    wp_hbm,
    wn_hbm,
    routes_ref,
    slots_ref,
    out_ref,
    kbuf,
    vbuf,
    wo,
    router,
    wd,
    wu,
    wg,
    wp,
    wn,
    hid,
    att,
    p_own,
    p_send,
    p_recv,
    res,
    n_all,
    lat_all,
    w_all,
    act,
    c_own,
    c_send,
    c_recv,
    d_send,
    d_recv,
    l_own,
    l_send,
    l_recv,
    kv_sem,
    w_sem,
    s1,
    r1,
    s2,
    r2,
    s3,
    r3,
    s3w,
    r3w,
    s4,
    r4,
    s5,
    r5,
    s6,
    r6,
    s7,
    r7,
):
    (T, E, R, r, D, NC, L, X, XA, F, N, TOPK, slots_all) = dims
    me = lax.axis_index("tp")
    ep = lax.axis_index("ep")
    CW = D // NC
    Hl, HD = q_ref.shape[1], q_ref.shape[2]
    G = nk_ref.shape[1]
    grp = Hl // G
    CACHE = k_hbm.shape[2]
    AC = 8
    NA = R // AC

    def tp_peer(k):
        return lax.rem(me + k, T)

    def ep_peer(i):
        return lax.rem(ep + i, E)

    def kv_copy(c, which):
        src, dst = ((k_hbm, kbuf), (v_hbm, vbuf))[which]
        rows = pl.ds(c * AC, AC)
        return pltpu.make_async_copy(src.at[rows], dst.at[rows], kv_sem.at[which, c])

    for c in range(NA):
        kv_copy(c, 0).start()
        kv_copy(c, 1).start()
    hid_copy = pltpu.make_async_copy(hidden_ref.at[me], hid, w_sem.at[0])
    loads = [
        pltpu.make_async_copy(src, dst, w_sem.at[i + 1])
        for i, (src, dst) in enumerate(
            (
                (wo_hbm, wo),
                (wd_hbm, wd),
                (router_hbm, router),
                (wg_hbm, wg),
                (wp_hbm, wp),
                (wn_hbm, wn),
                (wu_hbm, wu),
            )
        )
    ]
    loads[0].start()
    hid_copy.start()

    barrier = pltpu.get_barrier_semaphore()
    for k in range(1, T):
        pl.semaphore_signal(barrier, inc=1, device_id={"tp": tp_peer(k)}, device_id_type=MESH)
    for i in range(1, E):
        pl.semaphore_signal(barrier, inc=1, device_id={"ep": ep_peer(i)}, device_id_type=MESH)

    for load in loads[1:]:
        load.start()

    scale = 1.0 / math.sqrt(HD)

    def by_group(pieces, width):
        row = lax.broadcasted_iota(jnp.int32, (Hl, width), 0)
        value = jnp.broadcast_to(pieces[0], (Hl, width))
        for g in range(1, G):
            value = jnp.where(row >= g * grp, jnp.broadcast_to(pieces[g], (Hl, width)), value)
        return value

    def attend(c, carry):
        kv_copy(c, 0).wait()
        scores, owns = [], []
        column = lax.broadcasted_iota(jnp.int32, (Hl, CACHE), 1)
        for i in range(AC):
            s = c * AC + i
            qs = q_ref[s]
            sc = by_group([dot_nt(qs, kbuf[s, g]) for g in range(G)], CACHE) * scale
            scores.append(jnp.where(column < len_ref[s], sc, -jnp.inf))
            nks = nk_ref[s].astype(F32)
            nkx = by_group([nks[g : g + 1] for g in range(G)], HD)
            owns.append(jnp.sum(qs.astype(F32) * nkx, axis=-1, keepdims=True) * scale)
        kv_copy(c, 1).wait()
        probs, own_probs = [], []
        for i in range(AC):
            top = jnp.maximum(jnp.max(scores[i], axis=-1, keepdims=True), owns[i])
            expo = jnp.exp(scores[i] - top)
            own_expo = jnp.exp(owns[i] - top)
            total = jnp.sum(expo, axis=-1, keepdims=True) + own_expo
            probs.append((expo / total).astype(BF16))
            own_probs.append((own_expo / total).astype(BF16).astype(F32))
        for i in range(AC):
            s = c * AC + i
            mixed = by_group([dot(probs[i], vbuf[s, g]) for g in range(G)], HD)
            nvs = nv_ref[s].astype(F32)
            nvx = by_group([nvs[g : g + 1] for g in range(G)], HD)
            att[s] = mixed + own_probs[i] * nvx
        return carry

    lax.fori_loop(0, NA, attend, 0)
    attended = jnp.concatenate([att[:, h, :] for h in range(Hl)], axis=1).astype(BF16)

    pl.semaphore_wait(barrier, T - 1 + E - 1)

    def p_copy(c, k):
        peer = tp_peer(k)
        return pltpu.make_async_remote_copy(
            src_ref=p_send.at[c, peer],
            dst_ref=p_recv.at[c, k - 1],
            send_sem=s1.at[c, k - 1],
            recv_sem=r1.at[c, k - 1],
            device_id={"tp": peer},
            device_id_type=MESH,
        )

    loads[0].wait()

    def project(c, carry):
        cols = pl.ds(pl.multiple_of(c * CW, CW), CW)
        part = dot(attended, wo[:, cols]).reshape(T, r, CW)
        p_own[c] = part
        p_send[c] = part.astype(BF16)
        for k in range(1, T):
            p_copy(c, k).start()
        return carry

    lax.fori_loop(0, NC, project, 0)

    hid_copy.wait()
    sumsq = jnp.zeros((r, 1), F32)
    for c in range(NC):
        value = hid[:, c * CW : (c + 1) * CW].astype(F32) + p_own[c, me]
        for k in range(1, T):
            p_copy(c, k).wait_recv()
            value = value + p_recv[c, k - 1].astype(F32)
        res[c] = value
        sumsq = sumsq + jnp.sum(value * value, axis=-1, keepdims=True)
    inv = lax.rsqrt(sumsq * (1.0 / D) + 1e-05)
    for c in range(NC):
        gain = gain_ref[:, c * CW : (c + 1) * CW].astype(F32)
        n_all[me, c] = (res[c] * inv * gain).astype(BF16)

    def n_copy(k):
        peer = tp_peer(k)
        return pltpu.make_async_remote_copy(
            src_ref=n_all.at[me],
            dst_ref=n_all.at[me],
            send_sem=s2.at[k - 1],
            recv_sem=r2.at[k - 1],
            device_id={"tp": peer},
            device_id_type=MESH,
        )

    for k in range(1, T):
        n_copy(k).start()

    blk = pl.ds(pl.multiple_of(ep * R, R), R)
    ident = lax.broadcasted_iota(jnp.int32, (R, XA), 1)
    routes = routes_ref[blk, :]
    slots = slots_ref[blk, :]
    picked = jnp.zeros((R, XA), F32)
    kept = jnp.zeros((R, XA), F32)
    for k in range(TOPK):
        hit = jnp.where(routes[:, k : k + 1] == ident, 1.0, 0.0)
        picked = picked + hit
        kept = kept + jnp.where(slots[:, k : k + 1] < slots_all, hit, 0.0)

    loads[1].wait()
    loads[2].wait()
    for k in range(1, T):
        n_copy(k).wait_recv()
    pieces = [n_all[:, c].astype(F32).reshape(R, CW).astype(BF16) for c in range(NC)]
    latent = jnp.zeros((R, L), F32)
    for c in range(NC):
        latent = latent + dot(pieces[c], wd[c * CW : (c + 1) * CW, :])
    mine = pl.ds(pl.multiple_of(me * L, L), L)
    lat_all[blk, mine] = latent.astype(BF16)

    def lat_copy(i):
        return pltpu.make_async_remote_copy(
            src_ref=lat_all.at[blk, mine],
            dst_ref=lat_all.at[blk, mine],
            send_sem=s3.at[i - 1],
            recv_sem=r3.at[i - 1],
            device_id={"ep": ep_peer(i)},
            device_id_type=MESH,
        )

    def w_copy(i):
        return pltpu.make_async_remote_copy(
            src_ref=w_all.at[ep],
            dst_ref=w_all.at[ep],
            send_sem=s3w.at[i - 1],
            recv_sem=r3w.at[i - 1],
            device_id={"ep": ep_peer(i)},
            device_id_type=MESH,
        )

    def fwd_copy(i, k):
        rows = pl.ds(pl.multiple_of(ep_peer(E - i) * R, R), R)
        return pltpu.make_async_remote_copy(
            src_ref=lat_all.at[rows, mine],
            dst_ref=lat_all.at[rows, mine],
            send_sem=s4.at[i, k - 1],
            recv_sem=r4.at[i, k - 1],
            device_id={"tp": tp_peer(k)},
            device_id_type=MESH,
        )

    for i in range(1, E):
        lat_copy(i).start()
    for k in range(1, T):
        fwd_copy(0, k).start()

    logits = jnp.zeros((R, XA), F32)
    for c in range(NC):
        logits = logits + dot(pieces[c], router[c * CW : (c + 1) * CW, :])
    gates = jax.nn.sigmoid(logits)
    w_all[ep] = kept * gates / jnp.sum(picked * gates, axis=-1, keepdims=True)
    for i in range(1, E):
        w_copy(i).start()

    for i in range(1, E):
        lat_copy(i).wait_recv()
        for k in range(1, T):
            fwd_copy(i, k).start()
    for i in range(1, E):
        w_copy(i).wait_recv()
    for i in range(E):
        for k in range(1, T):
            fwd_copy(i, k).wait_recv()

    BR = 128 if N % 128 == 0 else R
    NB = N // BR
    per = BR // R
    for load in loads[3:]:
        load.wait()

    def expert(x, carry):
        def rows_step(b, carry):
            rows = pl.ds(pl.multiple_of(b * BR, BR), BR)
            lat = lat_all[rows, :]
            gate = dot(lat, wg[x])
            upper = dot(lat, wp[x])
            weights = w_all[pl.ds(b * per, per)].reshape(BR, XA)
            lane = lax.broadcasted_iota(jnp.int32, (BR, XA), 1)
            scaled = jnp.sum(
                jnp.where(lane == ep * X + x, weights, 0.0), axis=-1, keepdims=True
            )
            act[x, rows] = (jax.nn.silu(gate) * upper * scaled).astype(BF16)
            return carry

        return lax.fori_loop(0, NB, rows_step, carry)

    lax.fori_loop(0, X, expert, 0)

    def c_copy(k):
        return pltpu.make_async_remote_copy(
            src_ref=c_send.at[k - 1],
            dst_ref=c_recv.at[k - 1],
            send_sem=s5.at[k - 1],
            recv_sem=r5.at[k - 1],
            device_id={"tp": tp_peer(k)},
            device_id_type=MESH,
        )

    def down(k, b):
        rows = pl.ds(pl.multiple_of(b * BR, BR), BR)
        cols = pl.ds(pl.multiple_of(tp_peer(k) * L, L), L)
        value = dot(act[0, rows], wn[0, :, cols])
        for x in range(1, X):
            value = value + dot(act[x, rows], wn[x, :, cols])
        return rows, value

    for k in range(1, T):

        def send_rows(b, carry):
            rows, value = down(k, b)
            c_send[k - 1, rows] = value.astype(BF16)
            return carry

        lax.fori_loop(0, NB, send_rows, 0)
        c_copy(k).start()

    def own_rows(b, carry):
        rows, value = down(T, b)
        c_own[rows, :] = value
        return carry

    lax.fori_loop(0, NB, own_rows, 0)
    for k in range(1, T):
        c_copy(k).wait_recv()

    def d_copy(i):
        return pltpu.make_async_remote_copy(
            src_ref=d_send.at[ep_peer(i)],
            dst_ref=d_recv.at[i - 1],
            send_sem=s6.at[i - 1],
            recv_sem=r6.at[i - 1],
            device_id={"ep": ep_peer(i)},
            device_id_type=MESH,
        )

    def block_sum(j):
        rows = pl.ds(pl.multiple_of(j * R, R), R)
        value = c_own[rows, :]
        for k in range(1, T):
            value = value + c_recv[k - 1, rows].astype(F32)
        return value

    for i in range(1, E):
        d_send[ep_peer(i)] = block_sum(ep_peer(i)).astype(BF16)
        d_copy(i).start()
    combined = block_sum(ep)
    for i in range(1, E):
        d_copy(i).wait_recv()
        combined = combined + d_recv[i - 1].astype(F32)
    combined = combined.astype(BF16)

    def l_copy(c, k):
        peer = tp_peer(k)
        return pltpu.make_async_remote_copy(
            src_ref=l_send.at[c, peer],
            dst_ref=l_recv.at[c, k - 1],
            send_sem=s7.at[c, k - 1],
            recv_sem=r7.at[c, k - 1],
            device_id={"tp": peer},
            device_id_type=MESH,
        )

    def lift(c, carry):
        cols = pl.ds(pl.multiple_of(c * CW, CW), CW)
        part = dot(combined, wu[:, cols]).reshape(T, r, CW)
        l_own[c] = part
        l_send[c] = part.astype(BF16)
        for k in range(1, T):
            l_copy(c, k).start()
        return carry

    lax.fori_loop(0, NC, lift, 0)
    for c in range(NC):
        value = res[c] + l_own[c, me]
        for k in range(1, T):
            l_copy(c, k).wait_recv()
            value = value + l_recv[c, k - 1].astype(F32)
        out_ref[:, c * CW : (c + 1) * CW] = value.astype(BF16)

    for k in range(1, T):
        n_copy(k).wait_send()
        c_copy(k).wait_send()
        for c in range(NC):
            p_copy(c, k).wait_send()
            l_copy(c, k).wait_send()
        for i in range(E):
            fwd_copy(i, k).wait_send()
    for i in range(1, E):
        lat_copy(i).wait_send()
        w_copy(i).wait_send()
        d_copy(i).wait_send()


def on_device(
    hidden_in,
    queries,
    new_keys,
    new_values,
    key_cache,
    value_cache,
    lengths,
    out_weight,
    norm_gain,
    router_weight,
    latent_down,
    latent_up,
    gate_weight,
    up_weight,
    down_weight,
    routes,
    slot_index,
):
    T = lax.axis_size("tp")
    E = lax.axis_size("ep")
    R, Hl, HD = queries.shape
    D = hidden_in.shape[1]
    r = R // T
    L = latent_down.shape[1]
    LAT = L * T
    X, _, F = gate_weight.shape
    XA = router_weight.shape[1]
    N, TOPK = routes.shape
    slots_all = 2 * N * TOPK // XA
    NC = 4
    CW = D // NC
    dims = (T, E, R, r, D, NC, L, X, XA, F, N, TOPK, slots_all)
    vmem = pl.BlockSpec(memory_space=pltpu.VMEM)
    smem = pl.BlockSpec(memory_space=pltpu.SMEM)
    hbm = pl.BlockSpec(memory_space=pl.ANY)
    dma = pltpu.SemaphoreType.DMA
    scratch = [
        pltpu.VMEM(key_cache.shape, BF16),
        pltpu.VMEM(value_cache.shape, BF16),
        pltpu.VMEM(out_weight.shape, BF16),
        pltpu.VMEM(router_weight.shape, BF16),
        pltpu.VMEM(latent_down.shape, BF16),
        pltpu.VMEM(latent_up.shape, BF16),
        pltpu.VMEM(gate_weight.shape, BF16),
        pltpu.VMEM(up_weight.shape, BF16),
        pltpu.VMEM(down_weight.shape, BF16),
        pltpu.VMEM((r, D), BF16),
        pltpu.VMEM((R, Hl, HD), F32),
        pltpu.VMEM((NC, T, r, CW), F32),
        pltpu.VMEM((NC, T, r, CW), BF16),
        pltpu.VMEM((NC, T - 1, r, CW), BF16),
        pltpu.VMEM((NC, r, CW), F32),
        pltpu.VMEM((T, NC, r, CW), BF16),
        pltpu.VMEM((N, LAT), BF16),
        pltpu.VMEM((E, R, XA), F32),
        pltpu.VMEM((X, N, F), BF16),
        pltpu.VMEM((N, L), F32),
        pltpu.VMEM((T - 1, N, L), BF16),
        pltpu.VMEM((T - 1, N, L), BF16),

        pltpu.VMEM((E, R, L), BF16),
        pltpu.VMEM((E - 1, R, L), BF16),
        pltpu.VMEM((NC, T, r, CW), F32),
        pltpu.VMEM((NC, T, r, CW), BF16),
        pltpu.VMEM((NC, T - 1, r, CW), BF16),
        dma((2, R // 8)),
        dma((8,)),
        dma((NC, T - 1)),
        dma((NC, T - 1)),
        dma((T - 1,)),
        dma((T - 1,)),
        dma((E - 1,)),
        dma((E - 1,)),
        dma((E - 1,)),
        dma((E - 1,)),
        dma((E, T - 1)),
        dma((E, T - 1)),
        dma((T - 1,)),
        dma((T - 1,)),
        dma((E - 1,)),
        dma((E - 1,)),
        dma((NC, T - 1)),
        dma((NC, T - 1)),
    ]
    return pl.pallas_call(
        functools.partial(layer_kernel, dims),
        out_shape=jax.ShapeDtypeStruct((r, D), BF16),
        in_specs=[
            hbm,
            vmem,
            vmem,
            vmem,
            hbm,
            hbm,
            smem,
            hbm,
            vmem,
            hbm,
            hbm,
            hbm,
            hbm,
            hbm,
            hbm,
            vmem,
            vmem,
        ],
        out_specs=vmem,
        scratch_shapes=scratch,
        compiler_params=pltpu.CompilerParams(
            collective_id=0, has_side_effects=True, vmem_limit_bytes=60 * 1024 * 1024
        ),
    )(
        hidden_in.reshape(T, r, D),
        queries,
        new_keys,
        new_values,
        key_cache,
        value_cache,
        lengths,
        out_weight,
        norm_gain.reshape(1, D),
        router_weight,
        latent_down,
        latent_up,
        gate_weight,
        up_weight,
        down_weight,
        routes,
        slot_index,
    )


def solution(mesh):
    return jax.shard_map(
        on_device,
        mesh=mesh,
        in_specs=(
            P(("rep", "ep"), None),
            P(("rep", "ep"), "tp", None),
            P(("rep", "ep"), "tp", None),
            P(("rep", "ep"), "tp", None),
            P(("rep", "ep"), "tp", None, None),
            P(("rep", "ep"), "tp", None, None),
            P(("rep", "ep")),
            P("tp", None),
            P(),
            P(),
            P(None, "tp"),
            P("tp", None),
            P("ep", None, "tp"),
            P("ep", None, "tp"),
            P("ep", "tp", None),
            P("rep", None),
            P("rep", None),
        ),
        out_specs=P(("rep", "ep", "tp"), None),
        check_vma=False,
    )
```

time: 168 us -> 52 us (0.31)
  waiting for transfers between devices: 82.2 us -> 0 us
  Pallas kernels: 0 us -> 43.8 us
  matrix products: 32.2 us -> 0 us
  blocking collectives: 25 us -> 0 us
  between operations: 13.3 us -> 0.01 us
  other arithmetic: 5.82 us -> 0 us
  starting transfers between devices: 4.67 us -> 0 us
  local copies, waits for them, and re-layouts: 4.08 us -> 7.85 us
    reduce_scatter x3 -> x0, waiting for transfers between devices: 74.4 us -> none  [the longest x1 31.9 us: on_device(): lax.psum_scatter(jnp.einsum('jcf,jfl->ljc', active, down_weight, preferre...]
    pallas_call x0 -> x1, Pallas kernels: none -> 43.8 us  [on_device(): pl.pallas_call(functools.partial(layer_kernel, dims), out_shape=jax.Shape...]
    dot_general x12 -> x0, matrix products: 32.2 us -> none  [the longest x1 6.71 us: on_device(): jnp.einsum('jcf,jfl->ljc', active, down_weight, preferred_element_type=jn...]
    all_gather x3 -> x0, blocking collectives: 25 us -> none  [the longest x1 14 us: on_device(): lax.all_gather(latent_full, 'ep', axis=0, tiled=True)]
    all_to_all x1 -> x0, waiting for transfers between devices: 7.7 us -> none  [on_device(): lax.all_to_all(returned, 'ep', split_axis=1, concat_axis=1, tiled=True)]
    unnamed x16 -> x4, local copies, waits for them, and re-layouts: 1.32 us -> 6.55 us
    all_to_all x1 -> x0, starting transfers between devices: 4.62 us -> none  [on_device(): lax.all_to_all(returned, 'ep', split_axis=1, concat_axis=1, tiled=True)]
    convert_element_type x5 -> x0, other arithmetic: 3.28 us -> none  [the longest x1 1.52 us: on_device(): return (residual + lifted).astype(jnp.bfloat16)]
  transfers between devices with their start and end apart: 4 -> 0, of which waited for: 4 -> 0; matrix products, arithmetic and copies ran while one was open for 1% -> 0% of each run, Pallas kernels for 0% -> 0%
where the time goes in v1:
time: 52 us; the launch traced here: 51.7 us
  Pallas kernels  43.8 us (84%)
  local copies, waits for them, and re-layouts  7.85 us (15%)
    pallas_call x1, Pallas kernels, on_device(): pl.pallas_call(functools.partial(layer_kernel, dims), out_shape=jax.Shape...  43.8 us
    unnamed x4, local copies, waits for them, and re-layouts  6.55 us
    reshape x1, local copies, waits for them, and re-layouts, on_device(): norm_gain.reshape(1, D)  1.3 us

profile of v1, /device:TPU:0, one launch (start us, length us, event | category | flops | bytes accessed | tf_op | source)
XLA Modules:
  0.0 51.7 jit_solution(11813860836008870938)
XLA Ops:
  0.0 1.3 %reshape.7.gain_ref = bf16[1,4096]{1,0:T(2,128)(2,1)} reshape(bf16[4096]{0:T(1024)(128)(2,1)} %param.25) | data formatting | bytes 16384 | tf_op jit(solution)/shard_map/reshape | solution.py:563
  1.3 1.4 %copy.19.routes_ref = s32[128,16]{1,0:T(8,128)} copy(s32[128,16]{0,1:T(8,128)} %param.32) | data formatting | bytes 16384 | tf_op args[15]
  2.7 1.4 %copy.20.slots_ref = s32[128,16]{1,0:T(8,128)} copy(s32[128,16]{0,1:T(8,128)} %param.33) | data formatting | bytes 16384 | tf_op args[16]
  4.1 2.2 %copy.18.router_hbm = bf16[4096,16]{1,0:T(8,128)(2,1)} copy(bf16[4096,16]{0,1:T(8,128)(2,1)} %param.26) | data formatting | bytes 262144 | tf_op args[9]
  6.4 43.8 %shard_map.163 = bf16[8,4096]{1,0:T(8,128)(2,1)} custom-call(bf16[4,8,4096]{2,1,0:T(8,128)(2,1)} %bitcast.1, bf16[32,8,128]{2,1,0:T(8,128)(2,1)} %q_ref.1, bf16[32,2,128]{2,1,0:T(2,128)(2,1)} %nk_ref.1, bf16[32,2,128]{2,1,0:T(2,128)(2,1)} %nv_ref.1, bf16[32,2,256,128]{3,2,1,0:T(8,128)(2,1)} %k_hbm.1, bf16[32,2,256,128]{3,2,1,0:T(8,128)(2,1)} %v_hbm.1, ...), custom_call_target="tpu_custom_call" | custom-call | tf_op jit(solution)/shard_map/pallas_call | solution.py:527
  50.2 1.5 %copy.22 = bf16[8,4096]{1,0:T(8,128)(2,1)} copy(bf16[8,4096]{1,0:T(8,128)(2,1)} %shard_map.163) | data formatting | bytes 131072

commit v2 on v1

--- a/solution.py
+++ b/solution.py
@@ -58,7 +58,10 @@
     res,
     n_all,
     lat_all,
+    lat_mat,
     w_all,
+    picked_all,
+    kept_all,
     act,
     c_own,
     c_send,
@@ -206,6 +209,16 @@
 
     lax.fori_loop(0, NC, project, 0)
 
+    ident = lax.broadcasted_iota(jnp.int32, (XA, N), 0)
+    picked = jnp.zeros((XA, N), F32)
+    kept = jnp.zeros((XA, N), F32)
+    for k in range(TOPK):
+        hit = jnp.where(routes_ref[k : k + 1, :] == ident, 1.0, 0.0)
+        picked = picked + hit
+        kept = kept + jnp.where(slots_ref[k : k + 1, :] < slots_all, hit, 0.0)
+    picked_all[...] = picked.T
+    kept_all[...] = kept.T
+
     hid_copy.wait()
     sumsq = jnp.zeros((r, 1), F32)
     for c in range(NC):
@@ -217,7 +230,7 @@
         sumsq = sumsq + jnp.sum(value * value, axis=-1, keepdims=True)
     inv = lax.rsqrt(sumsq * (1.0 / D) + 1e-05)
     for c in range(NC):
-        gain = gain_ref[:, c * CW : (c + 1) * CW].astype(F32)
+        gain = gain_ref[c * CW : (c + 1) * CW].astype(F32).reshape(1, CW)
         n_all[me, c] = (res[c] * inv * gain).astype(BF16)
 
     def n_copy(k):
@@ -235,15 +248,8 @@
         n_copy(k).start()
 
     blk = pl.ds(pl.multiple_of(ep * R, R), R)
-    ident = lax.broadcasted_iota(jnp.int32, (R, XA), 1)
-    routes = routes_ref[blk, :]
-    slots = slots_ref[blk, :]
-    picked = jnp.zeros((R, XA), F32)
-    kept = jnp.zeros((R, XA), F32)
-    for k in range(TOPK):
-        hit = jnp.where(routes[:, k : k + 1] == ident, 1.0, 0.0)
-        picked = picked + hit
-        kept = kept + jnp.where(slots[:, k : k + 1] < slots_all, hit, 0.0)
+    picked = picked_all[blk, :]
+    kept = kept_all[blk, :]
 
     loads[1].wait()
     loads[2].wait()
@@ -253,13 +259,12 @@
     latent = jnp.zeros((R, L), F32)
     for c in range(NC):
         latent = latent + dot(pieces[c], wd[c * CW : (c + 1) * CW, :])
-    mine = pl.ds(pl.multiple_of(me * L, L), L)
-    lat_all[blk, mine] = latent.astype(BF16)
+    lat_all[me, ep] = latent.astype(BF16)
 
     def lat_copy(i):
         return pltpu.make_async_remote_copy(
-            src_ref=lat_all.at[blk, mine],
-            dst_ref=lat_all.at[blk, mine],
+            src_ref=lat_all.at[me, ep],
+            dst_ref=lat_all.at[me, ep],
             send_sem=s3.at[i - 1],
             recv_sem=r3.at[i - 1],
             device_id={"ep": ep_peer(i)},
@@ -277,10 +282,10 @@
         )
 
     def fwd_copy(i, k):
-        rows = pl.ds(pl.multiple_of(ep_peer(E - i) * R, R), R)
-        return pltpu.make_async_remote_copy(
-            src_ref=lat_all.at[rows, mine],
-            dst_ref=lat_all.at[rows, mine],
+        row = ep_peer(E - i)
+        return pltpu.make_async_remote_copy(
+            src_ref=lat_all.at[me, row],
+            dst_ref=lat_all.at[me, row],
             send_sem=s4.at[i, k - 1],
             recv_sem=r4.at[i, k - 1],
             device_id={"tp": tp_peer(k)},
@@ -294,7 +299,7 @@
 
     logits = jnp.zeros((R, XA), F32)
     for c in range(NC):
-        logits = logits + dot(pieces[c], router[c * CW : (c + 1) * CW, :])
+        logits = logits + dot_nt(pieces[c], router[:, c * CW : (c + 1) * CW])
     gates = jax.nn.sigmoid(logits)
     w_all[ep] = kept * gates / jnp.sum(picked * gates, axis=-1, keepdims=True)
     for i in range(1, E):
@@ -316,10 +321,13 @@
     for load in loads[3:]:
         load.wait()
 
+    for t in range(T):
+        lat_mat[:, t * L : (t + 1) * L] = lat_all[t].reshape(N, L)
+
     def expert(x, carry):
         def rows_step(b, carry):
             rows = pl.ds(pl.multiple_of(b * BR, BR), BR)
-            lat = lat_all[rows, :]
+            lat = lat_mat[rows, :]
             gate = dot(lat, wg[x])
             upper = dot(lat, wp[x])
             weights = w_all[pl.ds(b * per, per)].reshape(BR, XA)
@@ -480,7 +488,7 @@
         pltpu.VMEM(key_cache.shape, BF16),
         pltpu.VMEM(value_cache.shape, BF16),
         pltpu.VMEM(out_weight.shape, BF16),
-        pltpu.VMEM(router_weight.shape, BF16),
+        pltpu.VMEM((XA, D), BF16),
         pltpu.VMEM(latent_down.shape, BF16),
         pltpu.VMEM(latent_up.shape, BF16),
         pltpu.VMEM(gate_weight.shape, BF16),
@@ -493,8 +501,11 @@
         pltpu.VMEM((NC, T - 1, r, CW), BF16),
         pltpu.VMEM((NC, r, CW), F32),
         pltpu.VMEM((T, NC, r, CW), BF16),
+        pltpu.VMEM((T, E, R, L), BF16),
         pltpu.VMEM((N, LAT), BF16),
         pltpu.VMEM((E, R, XA), F32),
+        pltpu.VMEM((N, XA), F32),
+        pltpu.VMEM((N, XA), F32),
         pltpu.VMEM((X, N, F), BF16),
         pltpu.VMEM((N, L), F32),
         pltpu.VMEM((T - 1, N, L), BF16),
@@ -560,15 +571,15 @@
         value_cache,
         lengths,
         out_weight,
-        norm_gain.reshape(1, D),
-        router_weight,
+        norm_gain,
+        router_weight.T,
         latent_down,
         latent_up,
         gate_weight,
         up_weight,
         down_weight,
-        routes,
-        slot_index,
+        routes.T,
+        slot_index.T,
     )
 
 

time: 52 us -> 45.5 us (0.88)
  local copies, waits for them, and re-layouts: 7.85 us -> 1.47 us
    unnamed x4 -> x1, local copies, waits for them, and re-layouts: 6.55 us -> 1.47 us
    reshape x1 -> x0, local copies, waits for them, and re-layouts: 1.3 us -> none  [on_device(): norm_gain.reshape(1, D)]
where the time goes in v2:
time: 45.5 us; the launch traced here: 45.3 us
  Pallas kernels  43.8 us (96%)
  local copies, waits for them, and re-layouts  1.47 us (3%)
    pallas_call x1, Pallas kernels, on_device(): pl.pallas_call(functools.partial(layer_kernel, dims), out_shape=jax.Shape...  43.8 us
    unnamed x1, local copies, waits for them, and re-layouts  1.47 us

profile of v2, /device:TPU:0, one launch (start us, length us, event | category | flops | bytes accessed | tf_op | source)
XLA Modules:
  0.0 45.3 jit_solution(16099710281475580927)
XLA Ops:
  0.0 43.8 %shard_map.163 = bf16[8,4096]{1,0:T(8,128)(2,1)} custom-call(bf16[4,8,4096]{2,1,0:T(8,128)(2,1)} %bitcast.4, bf16[32,8,128]{2,1,0:T(8,128)(2,1)} %q_ref.1, bf16[32,2,128]{2,1,0:T(2,128)(2,1)} %nk_ref.1, bf16[32,2,128]{2,1,0:T(2,128)(2,1)} %nv_ref.1, bf16[32,2,256,128]{3,2,1,0:T(8,128)(2,1)} %k_hbm.1, bf16[32,2,256,128]{3,2,1,0:T(8,128)(2,1)} %v_hbm.1, ...), custom_call_target="tpu_custom_call" | custom-call | tf_op jit(solution)/shard_map/pallas_call | solution.py:538
  43.8 1.5 %copy.19 = bf16[8,4096]{1,0:T(8,128)(2,1)} copy(bf16[8,4096]{1,0:T(8,128)(2,1)} %shard_map.163) | data formatting | bytes 131072

commit v3 on v2

--- a/solution.py
+++ b/solution.py
@@ -142,6 +142,7 @@
     for load in loads[1:]:
         load.start()
 
+    far_first = sorted(range(1, T), key=lambda k: abs(2 * k - T))
     scale = 1.0 / math.sqrt(HD)
 
     def by_group(pieces, width):
@@ -203,7 +204,7 @@
         part = dot(attended, wo[:, cols]).reshape(T, r, CW)
         p_own[c] = part
         p_send[c] = part.astype(BF16)
-        for k in range(1, T):
+        for k in far_first:
             p_copy(c, k).start()
         return carry
 
@@ -244,7 +245,7 @@
             device_id_type=MESH,
         )
 
-    for k in range(1, T):
+    for k in far_first:
         n_copy(k).start()
 
     blk = pl.ds(pl.multiple_of(ep * R, R), R)
@@ -294,7 +295,7 @@
 
     for i in range(1, E):
         lat_copy(i).start()
-    for k in range(1, T):
+    for k in far_first:
         fwd_copy(0, k).start()
 
     logits = jnp.zeros((R, XA), F32)
@@ -307,7 +308,7 @@
 
     for i in range(1, E):
         lat_copy(i).wait_recv()
-        for k in range(1, T):
+        for k in far_first:
             fwd_copy(i, k).start()
     for i in range(1, E):
         w_copy(i).wait_recv()
@@ -360,7 +361,7 @@
             value = value + dot(act[x, rows], wn[x, :, cols])
         return rows, value
 
-    for k in range(1, T):
+    for k in far_first:
 
         def send_rows(b, carry):
             rows, value = down(k, b)
@@ -421,7 +422,7 @@
         part = dot(combined, wu[:, cols]).reshape(T, r, CW)
         l_own[c] = part
         l_send[c] = part.astype(BF16)
-        for k in range(1, T):
+        for k in far_first:
             l_copy(c, k).start()
         return carry
 
@@ -477,7 +478,7 @@
     XA = router_weight.shape[1]
     N, TOPK = routes.shape
     slots_all = 2 * N * TOPK // XA
-    NC = 4
+    NC = 2
     CW = D // NC
     dims = (T, E, R, r, D, NC, L, X, XA, F, N, TOPK, slots_all)
     vmem = pl.BlockSpec(memory_space=pltpu.VMEM)

time: 45.5 us -> 45.1 us (level)
  no operation moved by 1% of the time
where the time goes in v3:
time: 45.1 us; the launch traced here: 44.9 us
  Pallas kernels  43.5 us (96%)
  local copies, waits for them, and re-layouts  1.47 us (3%)
    pallas_call x1, Pallas kernels, on_device(): pl.pallas_call(functools.partial(layer_kernel, dims), out_shape=jax.Shape...  43.5 us
    unnamed x1, local copies, waits for them, and re-layouts  1.47 us

profile of v3, /device:TPU:0, one launch (start us, length us, event | category | flops | bytes accessed | tf_op | source)
XLA Modules:
  0.0 44.9 jit_solution(18164804422102076812)
XLA Ops:
  0.0 43.5 %shard_map.163 = bf16[8,4096]{1,0:T(8,128)(2,1)} custom-call(bf16[4,8,4096]{2,1,0:T(8,128)(2,1)} %bitcast.4, bf16[32,8,128]{2,1,0:T(8,128)(2,1)} %q_ref.1, bf16[32,2,128]{2,1,0:T(2,128)(2,1)} %nk_ref.1, bf16[32,2,128]{2,1,0:T(2,128)(2,1)} %nv_ref.1, bf16[32,2,256,128]{3,2,1,0:T(8,128)(2,1)} %k_hbm.1, bf16[32,2,256,128]{3,2,1,0:T(8,128)(2,1)} %v_hbm.1, ...), custom_call_target="tpu_custom_call" | custom-call | tf_op jit(solution)/shard_map/pallas_call | solution.py:539
  43.5 1.5 %copy.19 = bf16[8,4096]{1,0:T(8,128)(2,1)} copy(bf16[8,4096]{1,0:T(8,128)(2,1)} %shard_map.163) | data formatting | bytes 131072
